TPU v7x, 32 devices: a whole 2x2x4 slice. The times are simulated.
32 devices in a mesh: rep: 2 (over x), fsdp: 8 (over z, y), tp: 2 (over core).
Axes of the slice: x: 2, y: 2, z: 4, core: 2. Of those that a mesh axis runs over, the one named last changes fastest.
Arguments:
- states: bfloat16 [4, 32, 5120], P(None, 'rep', 'fsdp'), parts along dimension 1, may hold values from -24 to 24
- lengths: int32 [32], P(('rep', 'fsdp')), parts along dimension 0, may hold values from 1 to 512, as said below
- norm_gain: bfloat16 [5120], P('fsdp'), may hold values from 0.099609375 to 1.8984375
- query_weight: bfloat16 [5120, 8192], P('fsdp', 'tp'), may hold values from -0.078125 to 0.078125
- key_weight: bfloat16 [5120, 1024], P('fsdp', 'tp'), may hold values from -0.078125 to 0.078125
- value_weight: bfloat16 [5120, 1024], P('fsdp', 'tp'), may hold values from -0.078125 to 0.078125
- out_weight: bfloat16 [8192, 5120], P('tp', 'fsdp'), may hold values from -0.0625 to 0.0625
- query_down: bfloat16 [5120, 128], P('fsdp'), may hold values from -0.078125 to 0.078125
- query_up: bfloat16 [128, 8192], P('fsdp', 'tp'), may hold values from -0.5 to 0.5
- key_down: bfloat16 [5120, 128], P('fsdp'), may hold values from -0.078125 to 0.078125
- key_up: bfloat16 [128, 1024], P('fsdp', 'tp'), may hold values from -0.5 to 0.5
- value_down: bfloat16 [5120, 128], P('fsdp'), may hold values from -0.078125 to 0.078125
- value_up: bfloat16 [128, 1024], P('fsdp', 'tp'), may hold values from -0.5 to 0.5
- out_down: bfloat16 [8192, 128], P('tp', 'fsdp'), may hold values from -0.0625 to 0.0625
- out_up: bfloat16 [128, 5120], P(None, 'fsdp'), may hold values from -0.5 to 0.5
- key_cache: bfloat16 [32, 8, 512, 128], P(('rep', 'fsdp'), 'tp'), parts along dimension 0, may hold values from -260 to 260
- value_cache: bfloat16 [32, 8, 512, 128], P(('rep', 'fsdp'), 'tp'), parts along dimension 0, may hold values from -6 to 6
Outputs:
- next_states: bfloat16 [4, 32, 5120], P(None, 'rep', 'fsdp'), parts along dimension 1
There are 2 independent parts, one for each index of `rep`. A program takes and returns all parts, laid end to end along the dimension named above; an argument that names none is the same for every part. Nothing has to cross between parts.
Inputs may be any that keep to these rules, and one draw needn't show every extreme that they name: `lengths`: every value from 1 to 512 may occur, and both ends occur in every draw.
All inputs are finite; a program needn't handle non-finite values.
Results may differ from a plain program's by a relative error of at most 0.0078.
Values may be sent and summed in bfloat16 or wider, within the bound.
A program may use at most 64 MiB of HBM per device.

v0:
```python
import jax
import jax.numpy as jnp
from jax import lax
from jax.sharding import PartitionSpec as P

D = 5120
HD = 128


EPS = 1e-06


def rotate(block, positions):
    count = block.shape[0]
    heads = block.shape[1] // HD
    half = HD // 2
    freq = jnp.power(jnp.float32(1000000.0), -(2.0 * jnp.arange(half, dtype=jnp.float32)) / HD)
    angle = positions.astype(jnp.float32)[:, None] * freq[None, :]
    cosine = jnp.cos(angle)[:, None, :]
    sine = jnp.sin(angle)[:, None, :]
    shaped = block.reshape(count, heads, HD)
    first = shaped[:, :, :half]
    second = shaped[:, :, half:]
    turned = jnp.concatenate(
        [first * cosine - second * sine, second * cosine + first * sine], axis=2
    )
    return turned.reshape(count, heads * HD)


def split_heads(projected, query_cols, kv_cols, positions):
    count = projected.shape[0]
    kv_heads = kv_cols // HD
    group = query_cols // kv_cols
    queries = (
        rotate(projected[:, :query_cols], positions)
        .astype(jnp.bfloat16)
        .reshape(count, kv_heads, group, HD)
    )
    keys = (
        rotate(projected[:, query_cols : query_cols + kv_cols], positions)
        .astype(jnp.bfloat16)
        .reshape(count, kv_heads, HD)
    )
    values = projected[:, query_cols + kv_cols :].astype(jnp.bfloat16).reshape(count, kv_heads, HD)
    return (queries, keys, values)


def attend(queries, key_cache, value_cache, fresh_keys, fresh_values, lengths, step):
    count = queries.shape[0]
    factor = HD ** (-0.5)
    cached = (
        jnp.einsum("rkgd,rkcd->rkgc", queries, key_cache, preferred_element_type=jnp.float32)
        * factor
    )
    valid = jnp.arange(key_cache.shape[2], dtype=jnp.int32)[None, :] < lengths[:, None]
    cached = jnp.where(valid[:, None, None, :], cached, jnp.float32(-1e30))
    fresh = (
        jnp.einsum("rkgd,nrkd->rkgn", queries, fresh_keys, preferred_element_type=jnp.float32)
        * factor
    )
    live = jnp.arange(fresh_keys.shape[0], dtype=jnp.int32) <= step
    fresh = jnp.where(live[None, None, None, :], fresh, jnp.float32(-1e30))
    top = jnp.maximum(jnp.max(cached, axis=-1), jnp.max(fresh, axis=-1))
    cached_exp = jnp.exp(cached - top[..., None])
    fresh_exp = jnp.exp(fresh - top[..., None])
    total = jnp.sum(cached_exp, axis=-1) + jnp.sum(fresh_exp, axis=-1)
    cached_w = (cached_exp / total[..., None]).astype(jnp.bfloat16)
    fresh_w = (fresh_exp / total[..., None]).astype(jnp.bfloat16)
    mixed = jnp.einsum("rkgc,rkcd->rkgd", cached_w, value_cache, preferred_element_type=jnp.float32)
    mixed = mixed + jnp.einsum(
        "rkgn,nrkd->rkgd", fresh_w, fresh_values, preferred_element_type=jnp.float32
    )
    return mixed.astype(jnp.bfloat16).reshape(count, -1)


def body(
    states,
    lengths,
    norm_gain,
    query_weight,
    key_weight,
    value_weight,
    out_weight,
    query_down,
    query_up,
    key_down,
    key_up,
    value_down,
    value_up,
    out_down,
    out_up,
    key_cache,
    value_cache,
):
    wide = states.astype(jnp.float32)
    squares = jnp.sum(wide * wide, axis=2)
    totals = lax.psum(squares, "fsdp")
    normed = (wide * lax.rsqrt(totals / D + EPS)[..., None] * norm_gain.astype(jnp.float32)).astype(
        jnp.bfloat16
    )
    query_full, key_full, value_full, out_full = (
        lax.all_gather(query_up, "fsdp", axis=0, tiled=True),
        lax.all_gather(key_up, "fsdp", axis=0, tiled=True),
        lax.all_gather(value_up, "fsdp", axis=0, tiled=True),
        lax.all_gather(out_down, "fsdp", axis=1, tiled=True),
    )
    base = jnp.concatenate([query_weight, key_weight, value_weight], axis=1).astype(jnp.float32)
    delta = jnp.concatenate(
        [
            jnp.dot(query_down, query_full, preferred_element_type=jnp.float32),
            jnp.dot(key_down, key_full, preferred_element_type=jnp.float32),
            jnp.dot(value_down, value_full, preferred_element_type=jnp.float32),
        ],
        axis=1,
    )
    qkv_merged = (base + delta).astype(jnp.bfloat16)
    out_merged = (
        out_weight.astype(jnp.float32)
        + jnp.dot(out_full, out_up, preferred_element_type=jnp.float32)
    ).astype(jnp.bfloat16)
    query_cols = query_weight.shape[1]
    kv_cols = key_weight.shape[1]
    step_count = states.shape[0]
    row_total = states.shape[1]
    row_count = row_total // lax.axis_size("fsdp")
    kept_keys = []
    kept_values = []
    results = []
    for step in range(step_count):
        slab = normed[step]

        def project(start, count, slab=slab):
            return jnp.dot(slab, qkv_merged, preferred_element_type=jnp.float32)

        projected = lax.psum_scatter(
            project(jnp.int32(0), row_count * lax.axis_size("fsdp")),
            "fsdp",
            scatter_dimension=0,
            tiled=True,
        )
        queries, keys, values = split_heads(projected, query_cols, kv_cols, lengths + step)
        kept_keys.append(keys)
        kept_values.append(values)
        attended = attend(
            queries,
            key_cache,
            value_cache,
            jnp.stack(kept_keys),
            jnp.stack(kept_values),
            lengths,
            step,
        )
        partial_value = jnp.dot(
            lax.all_gather(attended, "fsdp", axis=0, tiled=True),
            out_merged,
            preferred_element_type=jnp.float32,
        )
        summed = lax.psum(partial_value, "tp")
        results.append((wide[step] + summed).astype(jnp.bfloat16))
    return jnp.stack(results)


def solution(mesh):
    in_specs = (
        P(None, "rep", "fsdp"),
        P(("rep", "fsdp")),
        P("fsdp"),
        P("fsdp", "tp"),
        P("fsdp", "tp"),
        P("fsdp", "tp"),
        P("tp", "fsdp"),
        P("fsdp", None),
        P("fsdp", "tp"),
        P("fsdp", None),
        P("fsdp", "tp"),
        P("fsdp", None),
        P("fsdp", "tp"),
        P("tp", "fsdp"),
        P(None, "fsdp"),
        P(("rep", "fsdp"), "tp", None, None),
        P(("rep", "fsdp"), "tp", None, None),
    )
    out_specs = P(None, "rep", "fsdp")
    return jax.shard_map(body, mesh=mesh, in_specs=in_specs, out_specs=out_specs, check_vma=False)
```

profile of v0, /device:TPU:0, one launch (start us, length us, event | category | flops | bytes accessed | tf_op | source)
XLA Modules:
  0.0 374.1 jit_solution(12101395777872245529)
XLA Ops:
  8.1 32.7 %all_gather.25 = bf16[128,512]{1,0:T(8,128)(2,1)S(1)} all-gather(bf16[16,512]{1,0:T(8,128)(2,1)} %param.27), channel_id=1, replica_groups=mesh['rep'=2,'fsdp'=8,'tp'=2] {'fsdp'}, dimensions={0}, use_global_device_ids=true | all-gather | bytes 147456 | tf_op jit(solution)/shard_map/all_gather | solution.py:103
  40.8 30.7 %all_gather.26 = bf16[128,512]{1,0:T(8,128)(2,1)S(1)} all-gather(bf16[16,512]{1,0:T(8,128)(2,1)} %param.29), channel_id=1, replica_groups=mesh['rep'=2,'fsdp'=8,'tp'=2] {'fsdp'}, dimensions={0}, use_global_device_ids=true | all-gather | bytes 147456 | tf_op jit(solution)/shard_map/all_gather | solution.py:104
  72.5 21.7 %psum.35 = f32[4,16]{1,0:T(4,128)S(1)} all-reduce(f32[4,16]{1,0:T(4,128)S(1)} %multiply_reduce_fusion), channel_id=1, replica_groups=mesh['rep'=2,'fsdp'=8,'tp'=2] {'fsdp'}, use_global_device_ids=true, to_apply=%region_1.0 | all-reduce | flops 64 | bytes 512 | tf_op jit(solution)/shard_map/psum | solution.py:97
  94.9 1.2 fusion.130
  96.2 2.3 fusion.131
  99.5 3.0 fusion.129
  102.5 3.9 %fusion = bf16[640,5120]{1,0:T(8,128)(2,1)S(1)} fusion(f32[640,512]{1,0:T(8,128)S(1)} %copy-done.2, f32[640,512]{1,0:T(8,128)S(1)} %fusion.130, f32[640,4096]{1,0:T(8,128)S(1)} %fusion.129, bf16[640,512]{1,0:T(8,128)(2,1)S(1)} %copy-done.4, bf16[640,512]{1,0:T(8,128)(2,1)S(1)} %copy-done.5, bf16[640,4096]{1,0:T(8,128)(2,1)} %param.20), kind=kLoop, calls=%fused_computation.1 | loop fusion | flops 32768000 | bytes 26214400 | tf_op jit(solution)/shard_map/convert_element_type | solution.py:116
  106.4 1.7 fusion.39
  108.1 1.8 fusion.40
  109.9 1.7 fusion.41
  111.6 1.7 fusion.42
  115.0 7.1 %add_convert_fusion = bf16[4096,640]{1,0:T(8,128)(2,1)} fusion(bf16[4096,640]{1,0:T(8,128)(2,1)} %param.23, bf16[4096,128]{0,1:T(8,128)(2,1)} %all-gather.9.cloned.1.call-done, bf16[128,640]{1,0:T(8,128)(2,1)S(1)} %copy-done.6), kind=kOutput, calls=%fused_computation.2 | convolution fusion | flops 678952960 | bytes 11698176 | tf_op jit(solution)/shard_map/dot_general | solution.py:119
  122.0 73.3 %all-reduce.9.cloned.1.call-done = (f32[16,5120]{1,0:T(8,128)}, f32[16,5120]{1,0:T(8,128)}, f32[16,5120]{1,0:T(8,128)}, f32[16,5120]{1,0:T(8,128)}) async-done(((f32[16,5120]{1,0:T(8,128)}, f32[16,5120]{1,0:T(8,128)}, f32[16,5120]{1,0:T(8,128)}, f32[16,5120]{1,0:T(8,128)}), (f32[16,5120]{1,0:T(8,128)}, f32[16,5120]{1,0:T(8,128)}, f32[16,5120]{1,0:T(8,128)}, ...) | async-done | bytes 1310736
  196.1 1.0 dynamic-slice_bitcast_fusion.2
  201.2 1.0 dynamic-slice_bitcast_fusion
  205.3 30.5 %all-gather = bf16[8,2,4096]{2,1,0:T(2,128)(2,1)S(1)} all-gather(bf16[1,2,4096]{2,1,0:T(2,128)(2,1)S(1)} %reshape.442), channel_id=1, replica_groups=mesh['rep'=2,'fsdp'=8,'tp'=2] {'fsdp'}, dimensions={0}, use_global_device_ids=true | all-gather | bytes 147456 | tf_op jit(solution)/shard_map/all_gather | solution.py:154
  237.7 30.7 %all-gather.1 = bf16[8,2,4096]{2,1,0:T(2,128)(2,1)S(1)} all-gather(bf16[1,2,4096]{2,1,0:T(2,128)(2,1)S(1)} %reshape.444), channel_id=1, replica_groups=mesh['rep'=2,'fsdp'=8,'tp'=2] {'fsdp'}, dimensions={0}, use_global_device_ids=true | all-gather | bytes 147456 | tf_op jit(solution)/shard_map/all_gather | solution.py:154
  268.4 3.9 %fusion.132 = f32[16,640]{1,0:T(8,128)} fusion(bf16[16,4096]{1,0:T(8,128)(2,1)S(1)} %reshape.443, bf16[4096,640]{1,0:T(8,128)(2,1)} %add_convert_fusion), kind=kOutput, calls=%fused_computation.223 | convolution fusion | flops 83886080 | bytes 5414912 | tf_op jit(solution)/shard_map/dot_general | solution.py:153
  272.3 3.9 %fusion.133 = f32[16,640]{1,0:T(8,128)} fusion(bf16[16,4096]{1,0:T(8,128)(2,1)S(1)} %reshape.445, bf16[4096,640]{1,0:T(8,128)(2,1)} %add_convert_fusion), kind=kOutput, calls=%fused_computation.224 | convolution fusion | flops 83886080 | bytes 5414912 | tf_op jit(solution)/shard_map/dot_general | solution.py:153
  277.8 30.6 %all-gather.2 = bf16[8,2,4096]{2,1,0:T(2,128)(2,1)S(1)} all-gather(bf16[1,2,4096]{2,1,0:T(2,128)(2,1)S(1)} %reshape.446), channel_id=1, replica_groups=mesh['rep'=2,'fsdp'=8,'tp'=2] {'fsdp'}, dimensions={0}, use_global_device_ids=true | all-gather | bytes 147456 | tf_op jit(solution)/shard_map/all_gather | solution.py:154
  308.5 3.9 %fusion.134 = f32[16,640]{1,0:T(8,128)} fusion(bf16[16,4096]{1,0:T(8,128)(2,1)S(1)} %reshape.447, bf16[4096,640]{1,0:T(8,128)(2,1)} %add_convert_fusion), kind=kOutput, calls=%fused_computation.225 | convolution fusion | flops 83886080 | bytes 5414912 | tf_op jit(solution)/shard_map/dot_general | solution.py:153
  314.1 30.5 %all-gather.3 = bf16[8,2,4096]{2,1,0:T(2,128)(2,1)S(1)} all-gather(bf16[1,2,4096]{2,1,0:T(2,128)(2,1)S(1)} %reshape.448), channel_id=1, replica_groups=mesh['rep'=2,'fsdp'=8,'tp'=2] {'fsdp'}, dimensions={0}, use_global_device_ids=true | all-gather | bytes 147456 | tf_op jit(solution)/shard_map/all_gather | solution.py:154
  344.7 3.9 %fusion.135 = f32[16,640]{1,0:T(8,128)} fusion(bf16[16,4096]{1,0:T(8,128)(2,1)S(1)} %reshape.449, bf16[4096,640]{1,0:T(8,128)(2,1)} %add_convert_fusion), kind=kOutput, calls=%fused_computation.226 | convolution fusion | flops 83886080 | bytes 5414912 | tf_op jit(solution)/shard_map/dot_general | solution.py:153
  348.6 17.4 %all-reduce.11.cloned.1.call-done = (f32[16,640]{1,0:T(8,128)}, f32[16,640]{1,0:T(8,128)}, f32[16,640]{1,0:T(8,128)}, f32[16,640]{1,0:T(8,128)}) async-done(((f32[16,640]{1,0:T(8,128)}, f32[16,640]{1,0:T(8,128)}, f32[16,640]{1,0:T(8,128)}, f32[16,640]{1,0:T(8,128)}), (f32[16,640]{1,0:T(8,128)}, f32[16,640]{1,0:T(8,128)}, f32[16,640]{1,0:T(8,128)}, f32[16,640]{1,0:T(8,128)})) %all-reduce.11.cloned.1.call-update) | async-done | bytes 163856 | tf_op jit(solution)/shard_map/psum | solution.py:158
  (118 shorter events, 19.8 us)
Async XLA Ops:
  6.5 197.7 %copy-start = (bf16[2,4,512,128]{3,2,1,0:T(8,128)(2,1)S(1)}, bf16[2,4,512,128]{3,2,1,0:T(8,128)(2,1)}, u32[]{:S(2)}) copy-start(bf16[2,4,512,128]{3,2,1,0:T(8,128)(2,1)} %param.32) | copy-start | bytes 3145732
  6.5 92.9 %all-gather.7.cloned.1.call-start = ((), (), s32[]{:S(2)}) async-start(), calls=%async_computation | async-start | bytes 1179648 | tf_op jit(solution)/shard_map/all_gather | solution.py:102
  7.3 107.7 %all-gather.9.cloned.1.call-start = ((), (), s32[]{:S(2)}) async-start(), calls=%async_computation.1 | async-start | bytes 1179648 | tf_op jit(solution)/shard_map/all_gather | solution.py:105
  8.0 187.3 %all-reduce.9.cloned.1.call-start = ((), (), s32[]{:S(2)}) async-start(), calls=%async_computation.2 | async-start | bytes 2621440
  99.4 3.0 copy-start.4
  99.5 3.0 copy-start.2
  99.5 3.0 copy-start.5
  109.9 3.5 copy-start.8
  109.9 4.8 %copy-start.7 = (s32[2]{0:T(128)S(1)}, s32[2]{0:T(128)}, u32[]{:S(2)}) copy-start(s32[2]{0:T(128)} %param.18) | copy-start | bytes 28
  109.9 5.0 %copy-start.6 = (bf16[128,640]{1,0:T(8,128)(2,1)S(1)}, bf16[128,640]{1,0:T(8,128)(2,1)}, u32[]{:S(2)}) copy-start(bf16[128,640]{1,0:T(8,128)(2,1)} %param.31) | copy-start | bytes 491524
  113.3 252.7 %all-reduce.11.cloned.1.call-start = ((), (), s32[]{:S(2)}) async-start(), calls=%async_computation.3 | async-start | bytes 327680 | tf_op jit(solution)/shard_map/psum | solution.py:158
  114.9 90.1 %copy-start.1 = (bf16[2,4,512,128]{3,2,1,0:T(8,128)(2,1)S(1)}, bf16[2,4,512,128]{3,2,1,0:T(8,128)(2,1)}, u32[]{:S(2)}) copy-start(bf16[2,4,512,128]{3,2,1,0:T(8,128)(2,1)} %param.33) | copy-start | bytes 3145732
  308.4 40.2 %copy-start.3 = (bf16[4,16,640]{2,1,0:T(8,128)(2,1)S(1)}, bf16[4,16,640]{2,1,0:T(8,128)(2,1)}, u32[]{:S(2)}) copy-start(bf16[4,16,640]{2,1,0:T(8,128)(2,1)} %param.17) | copy-start | bytes 245764
Sparse Core Ops, SparseCore 0:
  9.5 43.1 all-gather.6
  54.8 39.2 all-gather.8
  113.5 81.8 all-reduce.8
  348.7 17.2 all-reduce.10
where the time goes:
time: 375 us; the launch traced here: 374 us
  blocking collectives  207 us (55%)
  waiting for transfers between devices  92.2 us (25%)
  matrix products  40.8 us (11%)
  between operations  14.1 us (4%)
  other arithmetic  9.89 us (3%)
  local copies, waits for them, and re-layouts  9.46 us (3%)
    all_gather x4, blocking collectives, body(): lax.all_gather(attended, 'fsdp', axis=0, tiled=True)  122 us
    unnamed x5, waiting for transfers between devices  74.7 us
    all_gather x1, blocking collectives, body(): lax.all_gather(key_up, 'fsdp', axis=0, tiled=True)  32.7 us
    all_gather x1, blocking collectives, body(): lax.all_gather(value_up, 'fsdp', axis=0, tiled=True)  30.7 us
    psum x1, blocking collectives, body(): totals = lax.psum(squares, 'fsdp')  21.7 us
    psum x1, waiting for transfers between devices, body(): summed = lax.psum(partial_value, 'tp')  17.4 us
    dot_general x4, matrix products, body(): jnp.dot(lax.all_gather(attended, 'fsdp', axis=0, tiled=True), out_merged,...  15.6 us
  transfers between devices with their start and end apart: 4, of which 2 were waited for; matrix products, arithmetic and copies ran while one was open for 7% of the time, Pallas kernels for 0%

commit v1 on v0

--- a/solution.py
+++ b/solution.py
@@ -1,6 +1,12 @@
+import functools
+
 import jax
 import jax.numpy as jnp
+
+import numpy as np
 from jax import lax
+from jax.experimental import pallas as pl
+from jax.experimental.pallas import tpu as pltpu
 from jax.sharding import PartitionSpec as P
 
 D = 5120
@@ -160,6 +166,513 @@
     return jnp.stack(results)
 
 
+def fused_kernel(
+    cfg,
+    len_ref,
+    x_hbm,
+    gain_hbm,
+    qd_hbm,
+    kd_hbm,
+    vd_hbm,
+    qu_hbm,
+    ku_hbm,
+    vu_hbm,
+    od_hbm,
+    ou_hbm,
+    perm_hbm,
+    back_hbm,
+    freq_hbm,
+    qw_hbm,
+    kw_hbm,
+    vw_hbm,
+    ow_hbm,
+    kc_hbm,
+    vc_hbm,
+    out_ref,
+    x_ref,
+    gain_ref,
+    qd_ref,
+    kd_ref,
+    vd_ref,
+    qu_ref,
+    ku_ref,
+    vu_ref,
+    od_ref,
+    ou_ref,
+    perm_ref,
+    back_ref,
+    freq_ref,
+    w_buf,
+    ow_buf,
+    kc_buf,
+    vc_buf,
+    t_send,
+    t_recv,
+    p_send,
+    p_recv,
+    a_buf,
+    u_buf,
+    o_send,
+    o_recv,
+    s_sem,
+    w_sem,
+    ow_sem,
+    c_sem,
+    t_ssem,
+    t_rsem,
+    p_ssem,
+    p_rsem,
+    a_ssem,
+    a_rsem,
+    u_ssem,
+    u_rsem,
+    o_ssem,
+    o_rsem,
+):
+    n, tp, steps, rc = cfg
+    f32 = jnp.float32
+    bf16 = jnp.bfloat16
+    me = lax.axis_index("fsdp")
+    mt = lax.axis_index("tp")
+    rows = x_ref.shape[0]
+    m = steps * rc
+    chunk = kw_hbm.shape[1]
+    qn = qw_hbm.shape[1] // chunk
+    chunks = qn + 2
+    groups = chunks // 2
+    kv = chunk // HD
+    group = qn
+    rank = qu_ref.shape[0]
+
+    def peer(d):
+        return lax.rem(me + d, n)
+
+    def remote(src, dst, ssem, rsem, d, e=0):
+        return pltpu.make_async_remote_copy(
+            src_ref=src,
+            dst_ref=dst,
+            send_sem=ssem,
+            recv_sem=rsem,
+            device_id={"fsdp": peer(d), "tp": lax.rem(mt + e, tp)},
+            device_id_type=pl.DeviceIdType.MESH,
+        )
+
+    def weight_copy(c):
+        if c < qn:
+            src = qw_hbm.at[:, pl.ds(c * chunk, chunk)]
+        elif c == qn:
+            src = kw_hbm
+        else:
+            src = vw_hbm
+        return pltpu.make_async_copy(src, w_buf.at[c], w_sem.at[c])
+
+    small = [
+        pltpu.make_async_copy(src, dst, s_sem.at[i])
+        for i, (src, dst) in enumerate(
+            (
+                (perm_hbm, perm_ref),
+                (x_hbm, x_ref),
+                (gain_hbm, gain_ref),
+                (qd_hbm, qd_ref),
+                (kd_hbm, kd_ref),
+                (vd_hbm, vd_ref),
+                (qu_hbm, qu_ref),
+                (ku_hbm, ku_ref),
+                (vu_hbm, vu_ref),
+                (freq_hbm, freq_ref),
+                (back_hbm, back_ref),
+                (od_hbm, od_ref),
+                (ou_hbm, ou_ref),
+            )
+        )
+    ]
+    for copy in small:
+        copy.start()
+    order = []
+    for g in range(groups):
+        order += [g, groups + g]
+    loads = {}
+    for c in order:
+        loads[c] = weight_copy(c)
+        loads[c].start()
+    kc_load = pltpu.make_async_copy(kc_hbm, kc_buf, c_sem.at[0])
+    vc_load = pltpu.make_async_copy(vc_hbm, vc_buf, c_sem.at[1])
+    ow_load = pltpu.make_async_copy(ow_hbm, ow_buf, ow_sem)
+    kc_load.start()
+    vc_load.start()
+    ow_load.start()
+
+    barrier = pltpu.get_barrier_semaphore()
+    others = [(d, e) for e in range(tp) for d in range(n) if d or e]
+    for d, e in others:
+        pl.semaphore_signal(
+            barrier,
+            inc=1,
+            device_id={"fsdp": peer(d), "tp": lax.rem(mt + e, tp)},
+            device_id_type=pl.DeviceIdType.MESH,
+        )
+
+    for copy in small[:6]:
+        copy.wait()
+    xp = jnp.dot(perm_ref[...], x_ref[...], preferred_element_type=f32)
+    square = jnp.sum(xp[:rows] * xp[:rows], axis=1, keepdims=True)
+    xg = (xp * gain_ref[...].astype(f32)).astype(bf16)
+    lanes = xg.shape[0]
+    nt = (((0,), (1,)), ((), ()))
+    tt = [
+        lax.dot_general(ref[...], xg, nt, preferred_element_type=f32)
+        for ref in (qd_ref, kd_ref, vd_ref)
+    ]
+    for p in range(n):
+        for i in range(3):
+            t_send[p, i * rank : (i + 1) * rank, :] = tt[i][p * rank : (p + 1) * rank, :]
+        t_send[p, 3 * rank : 3 * rank + m, :] = jnp.broadcast_to(
+            square[p * m : (p + 1) * m], (m, lanes)
+        )
+    pl.semaphore_wait(barrier, len(others))
+    sends = []
+    t_copies = []
+    for d in range(1, n):
+        copy = remote(t_send.at[peer(d)], t_recv.at[d - 1], t_ssem.at[d - 1], t_rsem.at[d - 1], d)
+        copy.start()
+        t_copies.append(copy)
+        sends.append(copy)
+
+    xm = xg[:rows]
+
+    def base(c):
+        loads[c].wait()
+        return jnp.dot(xm, w_buf[c], preferred_element_type=f32)
+
+    first = [base(0), base(groups)]
+    for copy in small[6:9]:
+        copy.wait()
+    tsum = t_send[me]
+    for d in range(1, n):
+        t_copies[d - 1].wait_recv()
+        tsum = tsum + t_recv[d - 1]
+    low = [tsum[i * rank : (i + 1) * rank].astype(bf16) for i in range(3)]
+    scale = lax.rsqrt(tsum[3 * rank : 3 * rank + m] / D + EPS)
+    tn = (((0,), (0,)), ((), ()))
+
+    def delta(c):
+        if c < qn:
+            up, left = qu_ref[:, c * chunk : (c + 1) * chunk], low[0]
+        elif c == qn:
+            up, left = ku_ref[...], low[1]
+        else:
+            up, left = vu_ref[...], low[2]
+        return lax.dot_general(left, up, tn, preferred_element_type=f32)[:rows]
+
+    p_copies = []
+    for g in range(groups):
+        if g == 0:
+            lo, hi = first
+        else:
+            lo, hi = base(g), base(groups + g)
+        lo = lo + delta(g)
+        hi = hi + delta(groups + g)
+        both = jnp.concatenate(
+            [lo.reshape(n, m, chunk), hi.reshape(n, m, chunk)], axis=1
+        )
+        p_send[g] = both.astype(bf16)
+        for d in range(1, n):
+            copy = remote(
+                p_send.at[g, peer(d)],
+                p_recv.at[g, d - 1],
+                p_ssem.at[g, d - 1],
+                p_rsem.at[g, d - 1],
+                d,
+            )
+            copy.start()
+            p_copies.append(copy)
+            sends.append(copy)
+
+    for copy in small[9:]:
+        copy.wait()
+    index = lax.broadcasted_iota(jnp.int32, (m, HD), 0)
+    row = lax.rem(index, jnp.int32(rc))
+    position = lax.div(index, jnp.int32(rc))
+    for r in range(rc):
+        position = position + jnp.where(row == r, len_ref[r], 0)
+    angle = position.astype(f32) * freq_ref[0:1, :]
+    cosine = jnp.cos(angle)
+    sine = jnp.sin(angle) * freq_ref[1:2, :]
+
+    halves = [[], []]
+    k_next = 0
+    for g in range(groups):
+        total = p_send[g, me].astype(f32)
+        for d in range(1, n):
+            p_copies[k_next].wait_recv()
+            k_next += 1
+            total = total + p_recv[g, d - 1].astype(f32)
+        halves[0].append(total[:m])
+        halves[1].append(total[m:])
+    parts = halves[0] + halves[1]
+
+    def head(c, j):
+        return parts[c][:, j * HD : (j + 1) * HD] * scale[:, :HD]
+
+    def turned(block):
+        swapped = jnp.concatenate([block[:, HD // 2 :], block[:, : HD // 2]], axis=1)
+        return block * cosine + swapped * sine
+
+    kc_load.wait()
+    vc_load.wait()
+    factor = HD ** (-0.5)
+    q_rows = group * m
+    cache = kc_buf.shape[2]
+    q_index = lax.rem(lax.broadcasted_iota(jnp.int32, (q_rows, 1), 0), jnp.int32(m))
+    q_row = lax.rem(q_index, jnp.int32(rc))
+    q_step = lax.div(q_index, jnp.int32(rc))
+    limit = jnp.zeros((q_rows, 1), jnp.int32)
+    for r in range(rc):
+        limit = limit + jnp.where(q_row == r, len_ref[r], 0)
+    column = lax.broadcasted_iota(jnp.int32, (q_rows, cache), 1)
+    valid = column < limit
+    pad = 16
+    f_col = lax.broadcasted_iota(jnp.int32, (q_rows, pad), 1)
+    fresh_ok = (
+        (f_col < m)
+        & (lax.rem(f_col, jnp.int32(rc)) == q_row)
+        & (lax.div(f_col, jnp.int32(rc)) <= q_step)
+    )
+    nn = (((1,), (1,)), ((), ()))
+    zeros = jnp.zeros((pad - m, HD), f32)
+    heads = []
+    for k in range(kv):
+        tiles = []
+        for j in range(group):
+            h = k * group + j
+            tiles.append(turned(head(h // kv, h % kv)))
+        q = jnp.concatenate(tiles, axis=0).astype(bf16)
+        new_k = jnp.concatenate([turned(head(qn, k)), zeros], axis=0).astype(bf16)
+        new_v = jnp.concatenate([head(qn + 1, k), zeros], axis=0).astype(bf16)
+        score = jnp.zeros((q_rows, cache), f32)
+        for r in range(rc):
+            one = lax.dot_general(q, kc_buf[r, k], nn, preferred_element_type=f32)
+            score = jnp.where(q_row == r, one, score)
+        score = jnp.where(valid, score * factor, -1e30)
+        fresh = lax.dot_general(q, new_k, nn, preferred_element_type=f32) * factor
+        fresh = jnp.where(fresh_ok, fresh, -1e30)
+        top = jnp.maximum(
+            jnp.max(score, axis=1, keepdims=True), jnp.max(fresh, axis=1, keepdims=True)
+        )
+        e_score = jnp.exp(score - top)
+        e_fresh = jnp.exp(fresh - top)
+        inverse = 1.0 / (
+            jnp.sum(e_score, axis=1, keepdims=True) + jnp.sum(e_fresh, axis=1, keepdims=True)
+        )
+        weight = (e_score * inverse).astype(bf16)
+        mixed = jnp.dot(
+            (e_fresh * inverse).astype(bf16), new_v, preferred_element_type=f32
+        )
+        for r in range(rc):
+            one = jnp.dot(weight, vc_buf[r, k], preferred_element_type=f32)
+            mixed = mixed + jnp.where(q_row == r, one, 0.0)
+        for j in range(group):
+            heads.append(mixed[j * m : (j + 1) * m])
+    half = len(heads) // 2
+    both = jnp.concatenate(
+        [jnp.concatenate(heads[:half], axis=1), jnp.concatenate(heads[half:], axis=1)], axis=0
+    )
+    a_buf[me] = both.astype(bf16)
+    a_copies = []
+    for d in range(1, n):
+        copy = remote(a_buf.at[me], a_buf.at[me], a_ssem.at[d - 1], a_rsem.at[d - 1], d)
+        copy.start()
+        a_copies.append(copy)
+        sends.append(copy)
+    ow_load.wait()
+    for copy in a_copies:
+        copy.wait_recv()
+
+    flat = a_buf[...].reshape(n * 2 * m, -1)
+    lo = jnp.dot(back_ref[0], flat, preferred_element_type=f32).astype(bf16)
+    hi = jnp.dot(back_ref[1], flat, preferred_element_type=f32).astype(bf16)
+    split = lo.shape[1]
+    u = lax.dot_general(od_ref[:, :split], lo, nn, preferred_element_type=f32)
+    u = u + lax.dot_general(od_ref[:, split:], hi, nn, preferred_element_type=f32)
+    u_buf[mt, me] = u
+    u_copies = []
+    for i, (d, e) in enumerate(others):
+        copy = remote(
+            u_buf.at[mt, me], u_buf.at[mt, me], u_ssem.at[i], u_rsem.at[i], d, e
+        )
+        copy.start()
+        u_copies.append(copy)
+        sends.append(copy)
+    o_send[...] = jnp.dot(
+        lo[:rows], ow_buf[:split, :], preferred_element_type=f32
+    ) + jnp.dot(hi[:rows], ow_buf[split:, :], preferred_element_type=f32)
+    if tp > 1:
+        o_copy = remote(o_send, o_recv, o_ssem, o_rsem, 0, 1)
+        o_copy.start()
+        sends.append(o_copy)
+    for copy in u_copies:
+        copy.wait_recv()
+    whole = u_buf[0]
+    for t in range(1, tp):
+        whole = whole + u_buf[t]
+    whole = whole.reshape(n * rank, lanes).astype(bf16)
+    result = lax.dot_general(whole, ou_ref[...], tn, preferred_element_type=f32)[:rows]
+    result = result + x_ref[...].astype(f32)
+    if tp > 1:
+        o_copy.wait_recv()
+        result = result + (o_send[...] + o_recv[...])
+    else:
+        result = result + o_send[...]
+    out_ref[...] = result.astype(out_ref.dtype)
+    for copy in sends:
+        copy.wait_send()
+
+
+def fused(n, tp, *args):
+    (
+        states,
+        lengths,
+        norm_gain,
+        query_weight,
+        key_weight,
+        value_weight,
+        out_weight,
+        query_down,
+        query_up,
+        key_down,
+        key_up,
+        value_down,
+        value_up,
+        out_down,
+        out_up,
+        key_cache,
+        value_cache,
+    ) = args
+    steps, row_total, width = states.shape
+    rc = row_total // n
+    rows = steps * row_total
+    m = steps * rc
+    rank = query_up.shape[0]
+    chunk = key_weight.shape[1]
+    chunks = query_weight.shape[1] // chunk + 2
+    groups = chunks // 2
+    lanes = -(-rows // 128) * 128
+    bf16 = jnp.bfloat16
+    f32 = jnp.float32
+
+    perm = np.zeros((lanes, rows), np.float32)
+    back = np.zeros((2, lanes, n * 2 * m), np.float32)
+    for p in range(n):
+        for s in range(steps):
+            for r in range(rc):
+                natural = s * row_total + p * rc + r
+                perm[p * m + s * rc + r, natural] = 1
+                for side in range(2):
+                    back[side, natural, p * 2 * m + side * m + s * rc + r] = 1
+    half = HD // 2
+    freq = np.power(1000000.0, -(2.0 * np.arange(half)) / HD)
+    table = np.zeros((8, HD), np.float32)
+    table[0] = np.concatenate([freq, freq])
+    table[1] = np.concatenate([-np.ones(half), np.ones(half)])
+
+    vmem = pl.BlockSpec(memory_space=pltpu.VMEM)
+    smem = pl.BlockSpec(memory_space=pltpu.SMEM)
+    hbm = pl.BlockSpec(memory_space=pl.ANY)
+    dma = pltpu.SemaphoreType.DMA
+    att = query_weight.shape[1] // 2
+    out = pl.pallas_call(
+        functools.partial(fused_kernel, (n, tp, steps, rc)),
+        out_shape=jax.ShapeDtypeStruct((rows, width), states.dtype),
+        in_specs=[smem] + [hbm] * 19,
+        out_specs=vmem,
+        scratch_shapes=[
+            pltpu.VMEM((rows, width), bf16),
+            pltpu.VMEM((1, width), bf16),
+            pltpu.VMEM(query_down.shape, bf16),
+            pltpu.VMEM(key_down.shape, bf16),
+            pltpu.VMEM(value_down.shape, bf16),
+            pltpu.VMEM(query_up.shape, bf16),
+            pltpu.VMEM(key_up.shape, bf16),
+            pltpu.VMEM(value_up.shape, bf16),
+            pltpu.VMEM(out_down.shape[::-1], bf16),
+            pltpu.VMEM(out_up.shape, bf16),
+            pltpu.VMEM(perm.shape, bf16),
+            pltpu.VMEM(back.shape, bf16),
+            pltpu.VMEM(table.shape, f32),
+            pltpu.VMEM((chunks, width, chunk), bf16),
+            pltpu.VMEM(out_weight.shape, bf16),
+            pltpu.VMEM(key_cache.shape, bf16),
+            pltpu.VMEM(value_cache.shape, bf16),
+            pltpu.VMEM((n, 3 * rank + m, lanes), f32),
+            pltpu.VMEM((n - 1, 3 * rank + m, lanes), f32),
+            pltpu.VMEM((groups, n, 2 * m, chunk), bf16),
+            pltpu.VMEM((groups, n - 1, 2 * m, chunk), bf16),
+            pltpu.VMEM((n, 2 * m, att), bf16),
+            pltpu.VMEM((tp, n, rank, lanes), f32),
+            pltpu.VMEM((rows, width), f32),
+            pltpu.VMEM((rows, width), f32),
+            dma((13,)),
+            dma((chunks,)),
+            dma,
+            dma((2,)),
+            dma((n - 1,)),
+            dma((n - 1,)),
+            dma((groups, n - 1)),
+            dma((groups, n - 1)),
+            dma((n - 1,)),
+            dma((n - 1,)),
+            dma((n * tp - 1,)),
+            dma((n * tp - 1,)),
+            dma,
+            dma,
+        ],
+        compiler_params=pltpu.CompilerParams(
+            collective_id=0, has_side_effects=True, vmem_limit_bytes=56 * 2**20
+        ),
+    )(
+        lengths,
+        states.reshape(rows, width),
+        norm_gain.reshape(1, width),
+        query_down,
+        key_down,
+        value_down,
+        query_up,
+        key_up,
+        value_up,
+        out_down.T,
+        out_up,
+        jnp.asarray(perm, bf16),
+        jnp.asarray(back, bf16),
+        jnp.asarray(table),
+        query_weight,
+        key_weight,
+        value_weight,
+        out_weight,
+        key_cache,
+        value_cache,
+    )
+    return out.reshape(states.shape)
+
+
+def fits(n, tp, states, lengths, query_weight, key_weight, query_up):
+    m = states.shape[0] * lengths.shape[0]
+    return (
+        n > 1
+        and n <= 8
+        and tp == 2
+        and m == 8
+        and states.shape[2] % 128 == 0
+        and query_up.shape[0] % 16 == 0
+        and query_weight.shape[1] % (2 * key_weight.shape[1]) == 0
+    )
+
+
+def choose(n, tp, *args):
+    if fits(n, tp, args[0], args[1], args[3], args[4], args[8]):
+        return fused(n, tp, *args)
+    return body(*args)
+
+
 def solution(mesh):
     in_specs = (
         P(None, "rep", "fsdp"),
@@ -181,4 +694,4 @@
         P(("rep", "fsdp"), "tp", None, None),
     )
     out_specs = P(None, "rep", "fsdp")
-    return jax.shard_map(body, mesh=mesh, in_specs=in_specs, out_specs=out_specs, check_vma=False)
+    return jax.shard_map(functools.partial(choose, mesh.shape["fsdp"], mesh.shape["tp"]), mesh=mesh, in_specs=in_specs, out_specs=out_specs, check_vma=False)

time: 375 us -> 54.2 us (0.14)
  blocking collectives: 207 us -> 0 us
  waiting for transfers between devices: 92.2 us -> 0 us
  Pallas kernels: 0 us -> 51.2 us
  matrix products: 40.8 us -> 0 us
  between operations: 14.1 us -> 0.01 us
  other arithmetic: 9.89 us -> 0 us
  local copies, waits for them, and re-layouts: 9.46 us -> 2.79 us
    all_gather x6 -> x0, blocking collectives: 186 us -> none  [the longest x4 122 us: body(): lax.all_gather(attended, 'fsdp', axis=0, tiled=True)]
    unnamed x5 -> x0, waiting for transfers between devices: 74.7 us -> none
    pallas_call x0 -> x1, Pallas kernels: none -> 51.2 us  [fused(): pl.pallas_call(functools.partial(fused_kernel, (n, tp, steps, rc)), out_s...]
    dot_general x27 -> x0, matrix products: 40.8 us -> none  [the longest x4 15.6 us: body(): jnp.dot(lax.all_gather(attended, 'fsdp', axis=0, tiled=True), out_merged,...]
    psum x1 -> x0, blocking collectives: 21.7 us -> none  [body(): totals = lax.psum(squares, 'fsdp')]
    psum x1 -> x0, waiting for transfers between devices: 17.4 us -> none  [body(): summed = lax.psum(partial_value, 'tp')]
    slice x8 -> x0, local copies, waits for them, and re-layouts: 6.41 us -> none  [the longest x4 3.23 us: split_heads(): projected[:, query_cols:query_cols + kv_cols]]
    convert_element_type x5 -> x0, other arithmetic: 5.62 us -> none  [the longest x1 3.94 us: body(): qkv_merged = (base + delta).astype(jnp.bfloat16)]
  transfers between devices with their start and end apart: 4 -> 0, of which waited for: 2 -> 0; matrix products, arithmetic and copies ran while one was open for 7% -> 0% of each run, Pallas kernels for 0% -> 0%
where the time goes in v1:
time: 54.2 us; the launch traced here: 54 us
  Pallas kernels  51.2 us (94%)
  local copies, waits for them, and re-layouts  2.79 us (5%)
    pallas_call x1, Pallas kernels, fused(): pl.pallas_call(functools.partial(fused_kernel, (n, tp, steps, rc)), out_s...  51.2 us
    unnamed x1, local copies, waits for them, and re-layouts  1.53 us
    reshape x1, local copies, waits for them, and re-layouts, fused(): norm_gain.reshape(1, width)  1.26 us

profile of v1, /device:TPU:0, one launch (start us, length us, event | category | flops | bytes accessed | tf_op | source)
XLA Modules:
  0.0 54.0 jit_solution(17590174445623602883)
XLA Ops:
  0.0 1.3 %reshape.10.gain_hbm = bf16[1,640]{1,0:T(2,128)(2,1)} reshape(bf16[640]{0:T(1024)(128)(2,1)} %param.22) | data formatting | bytes 2560 | tf_op jit(solution)/shard_map/reshape | solution.py:635
  1.3 51.2 %shard_map.190 = bf16[64,640]{1,0:T(8,128)(2,1)} custom-call(s32[2]{0:T(128)} %len_ref.1, bf16[64,640]{1,0:T(8,128)(2,1)} %bitcast.5, bf16[1,640]{1,0:T(2,128)(2,1)} %reshape.10.gain_hbm, bf16[640,128]{1,0:T(8,128)(2,1)} %qd_hbm.1, bf16[640,128]{1,0:T(8,128)(2,1)} %kd_hbm.1, bf16[640,128]{1,0:T(8,128)(2,1)} %vd_hbm.1, bf16[16,4096]{1,0:T(8,128)(2,1)} %qu_hbm.1, ...), custom_call_target="tpu_custom_call" | custom-call | tf_op jit(solution)/shard_map/pallas_call | solution.py:583
  52.4 1.5 %copy.22 = bf16[4,16,640]{2,1,0:T(8,128)(2,1)} copy(bf16[4,16,640]{2,1,0:T(8,128)(2,1)} %bitcast.3) | data formatting | bytes 163840

commit v2 on v1

--- a/solution.py
+++ b/solution.py
@@ -209,6 +209,8 @@
     t_send,
     t_recv,
     p_send,
+    y_recv,
+    mid,
     p_recv,
     a_buf,
     u_buf,
@@ -220,6 +222,8 @@
     c_sem,
     t_ssem,
     t_rsem,
+    y_ssem,
+    y_rsem,
     p_ssem,
     p_rsem,
     a_ssem,
@@ -257,6 +261,21 @@
             device_id_type=pl.DeviceIdType.MESH,
         )
 
+    side_of = lax.rem(me, 2)
+    place = lax.div(me, 2)
+    far = n // 2
+    partner = me + 1 - 2 * side_of
+
+    def remote_to(src, dst, ssem, rsem, device):
+        return pltpu.make_async_remote_copy(
+            src_ref=src,
+            dst_ref=dst,
+            send_sem=ssem,
+            recv_sem=rsem,
+            device_id={"fsdp": device, "tp": mt},
+            device_id_type=pl.DeviceIdType.MESH,
+        )
+
     def weight_copy(c):
         if c < qn:
             src = qw_hbm.at[:, pl.ds(c * chunk, chunk)]
@@ -288,9 +307,8 @@
     ]
     for copy in small:
         copy.start()
-    order = []
-    for g in range(groups):
-        order += [g, groups + g]
+    pairs = [(qn, qn + 1)] + [(c, c + qn // 2) for c in range(qn // 2)]
+    order = [c for pair in pairs for c in pair]
     loads = {}
     for c in order:
         loads[c] = weight_copy(c)
@@ -316,7 +334,7 @@
         copy.wait()
     xp = jnp.dot(perm_ref[...], x_ref[...], preferred_element_type=f32)
     square = jnp.sum(xp[:rows] * xp[:rows], axis=1, keepdims=True)
-    xg = (xp * gain_ref[...].astype(f32)).astype(bf16)
+    xg = (xp * gain_ref[...].astype(f32).reshape(1, -1)).astype(bf16)
     lanes = xg.shape[0]
     nt = (((0,), (1,)), ((), ()))
     tt = [
@@ -327,7 +345,7 @@
         for i in range(3):
             t_send[p, i * rank : (i + 1) * rank, :] = tt[i][p * rank : (p + 1) * rank, :]
         t_send[p, 3 * rank : 3 * rank + m, :] = jnp.broadcast_to(
-            square[p * m : (p + 1) * m], (m, lanes)
+            square[(p % 2 * far + p // 2) * m : (p % 2 * far + p // 2 + 1) * m], (m, lanes)
         )
     pl.semaphore_wait(barrier, len(others))
     sends = []
@@ -344,7 +362,7 @@
         loads[c].wait()
         return jnp.dot(xm, w_buf[c], preferred_element_type=f32)
 
-    first = [base(0), base(groups)]
+    first = [base(c) for c in pairs[0]]
     for copy in small[6:9]:
         copy.wait()
     tsum = t_send[me]
@@ -365,28 +383,45 @@
         return lax.dot_general(left, up, tn, preferred_element_type=f32)[:rows]
 
     p_copies = []
+    y_copies = []
+
+    def spread(g):
+        y_copies[g].wait_recv()
+        joined = p_send[g, side_of].astype(f32) + y_recv[g].astype(f32)
+        mid[g] = joined.astype(bf16)
+        for d in range(1, far):
+            z = lax.rem(place + d, far)
+            copy = remote_to(
+                mid.at[g, z],
+                p_recv.at[g, d - 1],
+                p_ssem.at[g, d - 1],
+                p_rsem.at[g, d - 1],
+                2 * z + side_of,
+            )
+            copy.start()
+            p_copies.append(copy)
+            sends.append(copy)
+
     for g in range(groups):
         if g == 0:
             lo, hi = first
         else:
-            lo, hi = base(g), base(groups + g)
-        lo = lo + delta(g)
-        hi = hi + delta(groups + g)
+            lo, hi = base(pairs[g][0]), base(pairs[g][1])
+        lo = lo + delta(pairs[g][0])
+        hi = hi + delta(pairs[g][1])
         both = jnp.concatenate(
             [lo.reshape(n, m, chunk), hi.reshape(n, m, chunk)], axis=1
         )
-        p_send[g] = both.astype(bf16)
-        for d in range(1, n):
-            copy = remote(
-                p_send.at[g, peer(d)],
-                p_recv.at[g, d - 1],
-                p_ssem.at[g, d - 1],
-                p_rsem.at[g, d - 1],
-                d,
-            )
-            copy.start()
-            p_copies.append(copy)
-            sends.append(copy)
+        p_send[g] = both.astype(bf16).reshape(2, far, 2 * m, chunk)
+        copy = remote_to(
+            p_send.at[g, 1 - side_of], y_recv.at[g], y_ssem.at[g], y_rsem.at[g], partner
+        )
+        copy.start()
+        y_copies.append(copy)
+        sends.append(copy)
+        if g > 0:
+            spread(g - 1)
+    spread(groups - 1)
 
     for copy in small[9:]:
         copy.wait()
@@ -399,17 +434,15 @@
     cosine = jnp.cos(angle)
     sine = jnp.sin(angle) * freq_ref[1:2, :]
 
-    halves = [[], []]
-    k_next = 0
-    for g in range(groups):
-        total = p_send[g, me].astype(f32)
-        for d in range(1, n):
-            p_copies[k_next].wait_recv()
-            k_next += 1
+    parts = {}
+
+    def receive(g):
+        total = mid[g, place].astype(f32)
+        for d in range(1, far):
+            p_copies[g * (far - 1) + d - 1].wait_recv()
             total = total + p_recv[g, d - 1].astype(f32)
-        halves[0].append(total[:m])
-        halves[1].append(total[m:])
-    parts = halves[0] + halves[1]
+        parts[pairs[g][0]] = total[:m]
+        parts[pairs[g][1]] = total[m:]
 
     def head(c, j):
         return parts[c][:, j * HD : (j + 1) * HD] * scale[:, :HD]
@@ -440,8 +473,8 @@
     )
     nn = (((1,), (1,)), ((), ()))
     zeros = jnp.zeros((pad - m, HD), f32)
-    heads = []
-    for k in range(kv):
+
+    def attend_head(k):
         tiles = []
         for j in range(group):
             h = k * group + j
@@ -471,41 +504,75 @@
         for r in range(rc):
             one = jnp.dot(weight, vc_buf[r, k], preferred_element_type=f32)
             mixed = mixed + jnp.where(q_row == r, one, 0.0)
-        for j in range(group):
-            heads.append(mixed[j * m : (j + 1) * m])
-    half = len(heads) // 2
-    both = jnp.concatenate(
-        [jnp.concatenate(heads[:half], axis=1), jnp.concatenate(heads[half:], axis=1)], axis=0
-    )
-    a_buf[me] = both.astype(bf16)
-    a_copies = []
-    for d in range(1, n):
-        copy = remote(a_buf.at[me], a_buf.at[me], a_ssem.at[d - 1], a_rsem.at[d - 1], d)
+        return jnp.concatenate([mixed[j * m : (j + 1) * m] for j in range(group)], axis=1)
+
+    receive(0)
+    span = group // kv
+    sides = kv // 2
+    a_copies = {}
+
+    def block_to(i, owner, slot, device):
+        copy = remote_to(
+            a_buf.at[i, owner],
+            a_buf.at[i, owner],
+            a_ssem.at[i, slot],
+            a_rsem.at[i, slot],
+            device,
+        )
         copy.start()
-        a_copies.append(copy)
+        a_copies[i, slot] = copy
         sends.append(copy)
+
+    def forward(i):
+        for d in range(1, far):
+            a_copies[i, d - 1].wait_recv()
+            owner = 2 * lax.rem(place - d + far, far) + side_of
+            block_to(i, owner, far - 1 + d, partner)
+
+    for i in range(sides):
+        for j in range(span):
+            receive(1 + i * span + j)
+        both = jnp.concatenate([attend_head(i), attend_head(i + sides)], axis=0)
+        a_buf[i, me] = both.astype(bf16)
+        for d in range(1, far):
+            block_to(i, me, d - 1, 2 * lax.rem(place + d, far) + side_of)
+        block_to(i, me, far - 1, partner)
+        if i > 0:
+            forward(i - 1)
+    forward(sides - 1)
+
     ow_load.wait()
-    for copy in a_copies:
-        copy.wait_recv()
-
-    flat = a_buf[...].reshape(n * 2 * m, -1)
-    lo = jnp.dot(back_ref[0], flat, preferred_element_type=f32).astype(bf16)
-    hi = jnp.dot(back_ref[1], flat, preferred_element_type=f32).astype(bf16)
-    split = lo.shape[1]
-    u = lax.dot_general(od_ref[:, :split], lo, nn, preferred_element_type=f32)
-    u = u + lax.dot_general(od_ref[:, split:], hi, nn, preferred_element_type=f32)
-    u_buf[mt, me] = u
+    size = group * HD
+    u = jnp.zeros((rank, lanes), f32)
+    acc = jnp.zeros((rows, ow_buf.shape[1]), f32)
     u_copies = []
-    for i, (d, e) in enumerate(others):
-        copy = remote(
-            u_buf.at[mt, me], u_buf.at[mt, me], u_ssem.at[i], u_rsem.at[i], d, e
-        )
-        copy.start()
-        u_copies.append(copy)
-        sends.append(copy)
-    o_send[...] = jnp.dot(
-        lo[:rows], ow_buf[:split, :], preferred_element_type=f32
-    ) + jnp.dot(hi[:rows], ow_buf[split:, :], preferred_element_type=f32)
+    for i in range(sides):
+        for slot in range(far - 1, n - 1):
+            a_copies[i, slot].wait_recv()
+        flat = a_buf[i].reshape(n * 2 * m, size)
+        places = (i * size, (i + sides) * size)
+        cols = [
+            jnp.dot(back_ref[side], flat, preferred_element_type=f32).astype(bf16)
+            for side in range(2)
+        ]
+        for at, col in zip(places, cols):
+            u = u + lax.dot_general(
+                od_ref[:, at : at + size], col, nn, preferred_element_type=f32
+            )
+        if i == sides - 1:
+            u_buf[mt, me] = u
+            for j, (d, e) in enumerate(others):
+                copy = remote(
+                    u_buf.at[mt, me], u_buf.at[mt, me], u_ssem.at[j], u_rsem.at[j], d, e
+                )
+                copy.start()
+                u_copies.append(copy)
+                sends.append(copy)
+        for at, col in zip(places, cols):
+            acc = acc + jnp.dot(
+                col[:rows], ow_buf[at : at + size, :], preferred_element_type=f32
+            )
+    o_send[...] = acc
     if tp > 1:
         o_copy = remote(o_send, o_recv, o_ssem, o_rsem, 0, 1)
         o_copy.start()
@@ -566,7 +633,7 @@
         for s in range(steps):
             for r in range(rc):
                 natural = s * row_total + p * rc + r
-                perm[p * m + s * rc + r, natural] = 1
+                perm[(p % 2 * (n // 2) + p // 2) * m + s * rc + r, natural] = 1
                 for side in range(2):
                     back[side, natural, p * 2 * m + side * m + s * rc + r] = 1
     half = HD // 2
@@ -579,7 +646,8 @@
     smem = pl.BlockSpec(memory_space=pltpu.SMEM)
     hbm = pl.BlockSpec(memory_space=pl.ANY)
     dma = pltpu.SemaphoreType.DMA
-    att = query_weight.shape[1] // 2
+    kv = chunk // HD
+    size = query_weight.shape[1] // kv
     out = pl.pallas_call(
         functools.partial(fused_kernel, (n, tp, steps, rc)),
         out_shape=jax.ShapeDtypeStruct((rows, width), states.dtype),
@@ -587,7 +655,7 @@
         out_specs=vmem,
         scratch_shapes=[
             pltpu.VMEM((rows, width), bf16),
-            pltpu.VMEM((1, width), bf16),
+            pltpu.VMEM((width,), bf16),
             pltpu.VMEM(query_down.shape, bf16),
             pltpu.VMEM(key_down.shape, bf16),
             pltpu.VMEM(value_down.shape, bf16),
@@ -605,9 +673,11 @@
             pltpu.VMEM(value_cache.shape, bf16),
             pltpu.VMEM((n, 3 * rank + m, lanes), f32),
             pltpu.VMEM((n - 1, 3 * rank + m, lanes), f32),
-            pltpu.VMEM((groups, n, 2 * m, chunk), bf16),
-            pltpu.VMEM((groups, n - 1, 2 * m, chunk), bf16),
-            pltpu.VMEM((n, 2 * m, att), bf16),
+            pltpu.VMEM((groups, 2, n // 2, 2 * m, chunk), bf16),
+            pltpu.VMEM((groups, n // 2, 2 * m, chunk), bf16),
+            pltpu.VMEM((groups, n // 2, 2 * m, chunk), bf16),
+            pltpu.VMEM((groups, n // 2 - 1, 2 * m, chunk), bf16),
+            pltpu.VMEM((kv // 2, n, 2 * m, size), bf16),
             pltpu.VMEM((tp, n, rank, lanes), f32),
             pltpu.VMEM((rows, width), f32),
             pltpu.VMEM((rows, width), f32),
@@ -617,10 +687,12 @@
             dma((2,)),
             dma((n - 1,)),
             dma((n - 1,)),
-            dma((groups, n - 1)),
-            dma((groups, n - 1)),
-            dma((n - 1,)),
-            dma((n - 1,)),
+            dma((groups,)),
+            dma((groups,)),
+            dma((groups, n // 2 - 1)),
+            dma((groups, n // 2 - 1)),
+            dma((kv // 2, n - 1)),
+            dma((kv // 2, n - 1)),
             dma((n * tp - 1,)),
             dma((n * tp - 1,)),
             dma,
@@ -632,7 +704,7 @@
     )(
         lengths,
         states.reshape(rows, width),
-        norm_gain.reshape(1, width),
+        norm_gain,
         query_down,
         key_down,
         value_down,
@@ -657,12 +729,15 @@
 def fits(n, tp, states, lengths, query_weight, key_weight, query_up):
     m = states.shape[0] * lengths.shape[0]
     return (
-        n > 1
+        n > 2
+        and n % 2 == 0
         and n <= 8
         and tp == 2
         and m == 8
         and states.shape[2] % 128 == 0
         and query_up.shape[0] % 16 == 0
+        and key_weight.shape[1] % (2 * HD) == 0
+        and query_weight.shape[1] * HD % key_weight.shape[1] ** 2 == 0
         and query_weight.shape[1] % (2 * key_weight.shape[1]) == 0
     )
 

time: 54.2 us -> 47.5 us (0.88)
  Pallas kernels: 51.2 us -> 45.8 us
  local copies, waits for them, and re-layouts: 2.79 us -> 1.53 us
    pallas_call x1, Pallas kernels: 51.2 us -> 45.8 us  [fused(): pl.pallas_call(functools.partial(fused_kernel, (n, tp, steps, rc)), out_s...]
    reshape x1 -> x0, local copies, waits for them, and re-layouts: 1.26 us -> none  [fused(): norm_gain.reshape(1, width)]
where the time goes in v2:
time: 47.5 us; the launch traced here: 47.4 us
  Pallas kernels  45.8 us (96%)
  local copies, waits for them, and re-layouts  1.53 us (3%)
    pallas_call x1, Pallas kernels, fused(): pl.pallas_call(functools.partial(fused_kernel, (n, tp, steps, rc)), out_s...  45.8 us
    unnamed x1, local copies, waits for them, and re-layouts  1.53 us

profile of v2, /device:TPU:0, one launch (start us, length us, event | category | flops | bytes accessed | tf_op | source)
XLA Modules:
  0.0 47.4 jit_solution(3751418772929676918)
XLA Ops:
  0.0 45.8 %shard_map.190 = bf16[64,640]{1,0:T(8,128)(2,1)} custom-call(s32[2]{0:T(128)} %len_ref.1, bf16[64,640]{1,0:T(8,128)(2,1)} %bitcast.5, bf16[640]{0:T(1024)(128)(2,1)} %gain_hbm.1, bf16[640,128]{1,0:T(8,128)(2,1)} %qd_hbm.1, bf16[640,128]{1,0:T(8,128)(2,1)} %kd_hbm.1, bf16[640,128]{1,0:T(8,128)(2,1)} %vd_hbm.1, bf16[16,4096]{1,0:T(8,128)(2,1)} %qu_hbm.1, ...), custom_call_target="tpu_custom_call" | custom-call | tf_op jit(solution)/shard_map/pallas_call | solution.py:651
  45.9 1.5 %copy.22 = bf16[4,16,640]{2,1,0:T(8,128)(2,1)} copy(bf16[4,16,640]{2,1,0:T(8,128)(2,1)} %bitcast.3) | data formatting | bytes 163840
